TPU v7x, 32 devices: a whole 2x2x4 slice. The times are simulated.
32 devices in a mesh: blk: 8 (over z, y), group: 4 (over x, core).
Axes of the slice: x: 2, y: 2, z: 4, core: 2. Of those that a mesh axis runs over, the one named last changes fastest.
Arguments:
- frames: bfloat16 [4, 1024, 1024], P('group', 'blk'), may hold values from -6 to 6
- skip_in: bfloat16 [4, 1024, 1024], P('group', 'blk'), may hold values from -6 to 6
- lengths: int32 [4, 8], P('group'), may hold values from 1 to 957, as said below
- voiced: int32 [4, 8], P('group'), may hold values from 1 to 957, as said below
- time_steps: int32 [4, 8], P('group'), may hold values from 0 to 31
- time_table: bfloat16 [32, 1024], replicated, may hold values from -6 to 6
- skip_weight: bfloat16 [2048, 1024], replicated, may hold values from -0.125 to 0.125
- skip_bias: bfloat16 [1024], replicated, may hold values from -2 to 2
- adaptive_weight: bfloat16 [1024, 4096], replicated, may hold values from -0.1875 to 0.1875
- adaptive_bias: bfloat16 [4096], replicated, may hold values from -2 to 2
- merged_weight: bfloat16 [1024, 3072], replicated, may hold values from -0.1875 to 0.1875
- output_weight: bfloat16 [1024, 1024], replicated, may hold values from -2 to 2
- output_bias: bfloat16 [1024], replicated, may hold values from -2 to 2
- up_weight: bfloat16 [1024, 4096], replicated, may hold values from -0.1875 to 0.1875
- up_bias: bfloat16 [4096], replicated, may hold values from -2 to 2
- down_weight: bfloat16 [4096, 1024], replicated, may hold values from -0.09375 to 0.09375
- down_bias: bfloat16 [1024], replicated, may hold values from -2 to 2
- cotangent: bfloat16 [4, 1024, 1024], P('group', 'blk'), may hold values from -6 to 6
Outputs:
- layer_out: bfloat16 [4, 1024, 1024], P('group', 'blk')
- frames_grad: bfloat16 [4, 1024, 1024], P('group', 'blk')
- skip_grad: bfloat16 [4, 1024, 1024], P('group', 'blk')
- table_grad: float32 [32, 1024], P(None, 'blk')
- skip_weight_grad: float32 [2048, 1024], P('blk')
- skip_bias_grad: float32 [1024], P('blk')
- adaptive_weight_grad: float32 [1024, 4096], P('blk')
- adaptive_bias_grad: float32 [4096], P('blk')
- merged_weight_grad: float32 [1024, 3072], P('blk')
- output_weight_grad: float32 [1024, 1024], P('blk')
- output_bias_grad: float32 [1024], P('blk')
- up_weight_grad: float32 [1024, 4096], P('blk')
- up_bias_grad: float32 [4096], P('blk')
- down_weight_grad: float32 [4096, 1024], P('blk')
- down_bias_grad: float32 [1024], P('blk')
Inputs may be any that keep to these rules, and one draw needn't show every extreme that they name: In each group the lengths sum to 1024. One slot, at a place drawn from the seed, holds exactly the largest length; every other slot holds at most 16 frames. Each is at most the length of its slot and at least three quarters of it; the rest of the slot is padding that no query may attend to. The longest slot of a group is fully voiced.
All inputs are finite; a program needn't handle non-finite values.
Results may differ from a plain program's by a relative error of at most 0.022.
Values may be sent and summed in bfloat16 or wider, within the bound.
A program may use at most 256 MiB of HBM per device.

v0:
```python
import math

import jax
import jax.numpy as jnp
from jax import lax
from jax.sharding import PartitionSpec as P

HEADS = 16
HD = 64


EPSILON = 1e-06
SCALE = 0.125
HIGHEST = lax.Precision.HIGHEST


def frame_facts(lengths, voiced, position):
    ends = jnp.cumsum(lengths)
    begins = ends - lengths
    segment = jnp.sum((position[:, None] >= ends[None, :]).astype(jnp.int32), axis=1)
    member = segment[:, None] == jnp.arange(lengths.shape[0], dtype=jnp.int32)[None, :]
    offset = position - jnp.sum(jnp.where(member, begins[None, :], 0), axis=1)
    limit = jnp.sum(jnp.where(member, voiced[None, :], 0), axis=1)
    return (segment, offset, offset < limit, member.astype(jnp.float32))


def turn_tables(offset, head_size):
    half = head_size // 2
    freq = 10000.0 ** (-jnp.arange(half, dtype=jnp.float32) * 2.0 / head_size)
    angle = offset.astype(jnp.float32)[:, None] * freq[None, :]
    return (jnp.cos(angle), jnp.sin(angle))


def rotate(values, cosine, sine):
    half = values.shape[-1] // 2
    front = values[..., :half]
    behind = values[..., half:]
    cos_part = cosine[:, None, :]
    sin_part = sine[:, None, :]
    return jnp.concatenate(
        [front * cos_part - behind * sin_part, behind * cos_part + front * sin_part], axis=-1
    )


def adaptive_norm(hidden, scale, shift):
    mean = jnp.mean(hidden, axis=-1, keepdims=True)
    centred = hidden - mean
    variance = jnp.mean(centred * centred, axis=-1, keepdims=True)
    return centred * lax.rsqrt(variance + EPSILON) * (1.0 + scale) + shift


def weights_of(query_rows, key_rows, mask):
    scores = (
        jnp.einsum("qhd,khd->hqk", query_rows, key_rows, preferred_element_type=jnp.float32) * SCALE
    )
    return jnp.where(mask[None, :, :], jnp.exp(scores), 0.0)


def over_blocks(count, step_fn, carry):
    block = math.gcd(count, 512)

    def advance(index, state):
        return step_fn(state, index * block, block)

    return lax.fori_loop(0, count // block, advance, carry)


def on_device(
    frames,
    skip_in,
    lengths,
    voiced,
    time_steps,
    time_table,
    skip_weight,
    skip_bias,
    adaptive_weight,
    adaptive_bias,
    merged_weight,
    output_weight,
    output_bias,
    up_weight,
    up_bias,
    down_weight,
    down_bias,
    cotangent,
):
    rows = frames.shape[1]
    width = frames.shape[2]
    lengths_here = lengths[0]
    voiced_here = voiced[0]
    device = lax.axis_index("blk")
    position = device * rows + jnp.arange(rows, dtype=jnp.int32)
    segment, offset, valid, member = frame_facts(lengths_here, voiced_here, position)
    cosine, sine = turn_tables(offset, HD)

    def key_mask(first_frame, count):
        key_position = first_frame + jnp.arange(count, dtype=jnp.int32)
        key_segment, key_offset, key_valid, key_member = frame_facts(
            lengths_here, voiced_here, key_position
        )
        return (segment[:, None] == key_segment[None, :]) & key_valid[None, :]

    def query_mask(first_frame, count):
        query_position = first_frame + jnp.arange(count, dtype=jnp.int32)
        query_segment, query_offset, query_valid, query_member = frame_facts(
            lengths_here, voiced_here, query_position
        )
        return (query_segment[:, None] == segment[None, :]) & valid[None, :]

    step_hot = (
        time_steps[0][:, None] == jnp.arange(time_table.shape[0], dtype=jnp.int32)[None, :]
    ).astype(jnp.float32)
    embed = jnp.dot(step_hot, time_table.astype(jnp.float32), precision=HIGHEST)
    cond, silu_back = jax.vjp(jax.nn.silu, embed)
    cond_low = cond.astype(jnp.bfloat16)
    per_utterance = jnp.dot(
        cond_low, adaptive_weight, preferred_element_type=jnp.float32
    ) + adaptive_bias.astype(jnp.float32)
    modulate = jnp.dot(member, per_utterance, precision=HIGHEST)
    joined = jnp.concatenate([frames[0], skip_in[0]], axis=1)
    first = jnp.dot(joined, skip_weight, preferred_element_type=jnp.float32) + skip_bias.astype(
        jnp.float32
    )
    normed, norm_back = jax.vjp(
        adaptive_norm, first, modulate[:, :width], modulate[:, width : 2 * width]
    )
    normed_low = normed.astype(jnp.bfloat16)
    merged = jnp.dot(normed_low, merged_weight, preferred_element_type=jnp.float32)
    query3 = rotate(merged[:, :width].reshape(rows, HEADS, HD), cosine, sine).astype(jnp.bfloat16)
    key3 = rotate(merged[:, width : 2 * width].reshape(rows, HEADS, HD), cosine, sine).astype(
        jnp.bfloat16
    )
    value3 = merged[:, 2 * width :].reshape(rows, HEADS, HD).astype(jnp.bfloat16)
    queries = query3.reshape(rows, width)
    keys = key3.reshape(rows, width)
    values = value3.reshape(rows, width)
    empty_rows = jnp.zeros((rows, width), jnp.float32)
    empty_heads = jnp.zeros((HEADS, rows), jnp.float32)
    piece_keys = lax.all_gather(keys, "blk", axis=0, tiled=True)
    piece_values = lax.all_gather(values, "blk", axis=0, tiled=True)

    def forward_add_block(state, inner, block):
        numer, total = state
        key_rows = lax.dynamic_slice_in_dim(piece_keys, inner, block, 0).reshape(block, HEADS, HD)
        value_rows = lax.dynamic_slice_in_dim(piece_values, inner, block, 0).reshape(
            block, HEADS, HD
        )
        expo = weights_of(query3, key_rows, key_mask(inner, block))
        total = total + jnp.sum(expo, axis=2)
        numer = numer + jnp.einsum(
            "hqk,khd->qhd",
            expo.astype(jnp.bfloat16),
            value_rows,
            preferred_element_type=jnp.float32,
        ).reshape(rows, width)
        return (numer, total)

    numer, total = over_blocks(piece_keys.shape[0], forward_add_block, (empty_rows, empty_heads))
    mixed3 = numer.reshape(rows, HEADS, HD) / jnp.transpose(total)[:, :, None]
    mixed_low = mixed3.reshape(rows, width).astype(jnp.bfloat16)
    attended = jnp.dot(
        mixed_low, output_weight, preferred_element_type=jnp.float32
    ) + output_bias.astype(jnp.float32)
    second = first + attended
    normed_two, norm_two_back = jax.vjp(
        adaptive_norm, second, modulate[:, 2 * width : 3 * width], modulate[:, 3 * width :]
    )
    normed_two_low = normed_two.astype(jnp.bfloat16)
    hidden = jnp.dot(
        normed_two_low, up_weight, preferred_element_type=jnp.float32
    ) + up_bias.astype(jnp.float32)
    activated, gelu_back = jax.vjp(jax.nn.gelu, hidden)
    activated_low = activated.astype(jnp.bfloat16)
    result = (
        second
        + jnp.dot(activated_low, down_weight, preferred_element_type=jnp.float32)
        + down_bias.astype(jnp.float32)
    )
    layer_out = result.astype(jnp.bfloat16)
    outer_grad = cotangent[0]
    outer_float = outer_grad.astype(jnp.float32)
    down_weight_term = jnp.einsum(
        "rf,rd->fd", activated_low, outer_grad, preferred_element_type=jnp.float32
    )
    down_bias_term = jnp.sum(outer_float, axis=0)
    grad_act = jnp.einsum("rd,fd->rf", outer_grad, down_weight, preferred_element_type=jnp.float32)
    (grad_hidden,) = gelu_back(grad_act)
    grad_hidden_low = grad_hidden.astype(jnp.bfloat16)
    up_weight_term = jnp.einsum(
        "rd,rf->df", normed_two_low, grad_hidden_low, preferred_element_type=jnp.float32
    )
    up_bias_term = jnp.sum(grad_hidden_low.astype(jnp.float32), axis=0)
    grad_normed_two = jnp.einsum(
        "rf,df->rd", grad_hidden_low, up_weight, preferred_element_type=jnp.float32
    )
    grad_second_norm, grad_scale_two, grad_shift_two = norm_two_back(grad_normed_two)
    grad_second = outer_float + grad_second_norm
    grad_attended = grad_second.astype(jnp.bfloat16)
    output_weight_term = jnp.einsum(
        "rd,re->de", mixed_low, grad_attended, preferred_element_type=jnp.float32
    )
    output_bias_term = jnp.sum(grad_attended.astype(jnp.float32), axis=0)
    grad_mixed3 = jnp.einsum(
        "re,de->rd", grad_attended, output_weight, preferred_element_type=jnp.float32
    ).reshape(rows, HEADS, HD)
    pull3 = (grad_mixed3 / jnp.transpose(total)[:, :, None]).astype(jnp.bfloat16)
    pulls = pull3.reshape(rows, width)
    correction = -jnp.transpose(jnp.sum(grad_mixed3 * mixed3, axis=2)) / total
    query_piece_keys = lax.all_gather(keys, "blk", axis=0, tiled=True)
    query_piece_values = lax.all_gather(values, "blk", axis=0, tiled=True)

    def query_add_block(state, inner, block):
        key_rows = lax.dynamic_slice_in_dim(query_piece_keys, inner, block, 0).reshape(
            block, HEADS, HD
        )
        value_rows = lax.dynamic_slice_in_dim(query_piece_values, inner, block, 0).reshape(
            block, HEADS, HD
        )
        expo = weights_of(query3, key_rows, key_mask(inner, block))
        pushed = jnp.einsum("qhd,khd->hqk", pull3, value_rows, preferred_element_type=jnp.float32)
        slope = (expo * (pushed + correction[:, :, None]) * SCALE).astype(jnp.bfloat16)
        return state + jnp.einsum(
            "hqk,khd->qhd", slope, key_rows, preferred_element_type=jnp.float32
        ).reshape(rows, width)

    grad_query = over_blocks(query_piece_keys.shape[0], query_add_block, empty_rows)
    corrections_all = lax.all_gather(correction, "blk", axis=1, tiled=True)
    piece_queries = lax.all_gather(queries, "blk", axis=0, tiled=True)
    piece_pulls = lax.all_gather(pulls, "blk", axis=0, tiled=True)

    def key_add_block(state, inner, block):
        grad_keys, grad_values = state
        query_rows = lax.dynamic_slice_in_dim(piece_queries, inner, block, 0).reshape(
            block, HEADS, HD
        )
        pull_rows = lax.dynamic_slice_in_dim(piece_pulls, inner, block, 0).reshape(block, HEADS, HD)
        expo = weights_of(query_rows, key3, query_mask(inner, block))
        pushed = jnp.einsum("qhd,khd->hqk", pull_rows, value3, preferred_element_type=jnp.float32)
        row_terms = lax.dynamic_slice_in_dim(corrections_all, inner, block, 1)
        slope = (expo * (pushed + row_terms[:, :, None]) * SCALE).astype(jnp.bfloat16)
        grad_keys = grad_keys + jnp.einsum(
            "hqk,qhd->khd", slope, query_rows, preferred_element_type=jnp.float32
        ).reshape(rows, width)
        grad_values = grad_values + jnp.einsum(
            "hqk,qhd->khd", expo.astype(jnp.bfloat16), pull_rows, preferred_element_type=jnp.float32
        ).reshape(rows, width)
        return (grad_keys, grad_values)

    grad_keys, grad_values = over_blocks(
        piece_queries.shape[0], key_add_block, (empty_rows, empty_rows)
    )
    query_back = rotate(grad_query.reshape(rows, HEADS, HD), cosine, -sine).reshape(rows, width)
    key_back = rotate(grad_keys.reshape(rows, HEADS, HD), cosine, -sine).reshape(rows, width)
    grad_merged = jnp.concatenate([query_back, key_back, grad_values], axis=1).astype(jnp.bfloat16)
    merged_weight_term = jnp.einsum(
        "rd,re->de", normed_low, grad_merged, preferred_element_type=jnp.float32
    )
    grad_normed = jnp.einsum(
        "re,de->rd", grad_merged, merged_weight, preferred_element_type=jnp.float32
    )
    grad_first_norm, grad_scale_one, grad_shift_one = norm_back(grad_normed)
    grad_first = (grad_second + grad_first_norm).astype(jnp.bfloat16)
    skip_weight_term = jnp.einsum(
        "rc,rd->cd", joined, grad_first, preferred_element_type=jnp.float32
    )
    skip_bias_term = jnp.sum(grad_first.astype(jnp.float32), axis=0)
    grad_joined = jnp.einsum(
        "rd,cd->rc", grad_first, skip_weight, preferred_element_type=jnp.float32
    )
    frames_grad = grad_joined[:, :width].astype(jnp.bfloat16)
    skip_grad = grad_joined[:, width:].astype(jnp.bfloat16)
    frame_modulate = jnp.concatenate(
        [grad_scale_one, grad_shift_one, grad_scale_two, grad_shift_two], axis=1
    )
    grad_modulate = jnp.dot(jnp.transpose(member), frame_modulate, precision=HIGHEST)
    adaptive_weight_term = jnp.dot(
        jnp.transpose(cond_low.astype(jnp.float32)), grad_modulate, precision=HIGHEST
    )
    adaptive_bias_term = jnp.sum(grad_modulate, axis=0)
    grad_cond = jnp.dot(
        grad_modulate,
        jnp.transpose(adaptive_weight),
        precision=HIGHEST,
        preferred_element_type=jnp.float32,
    )
    (grad_embed,) = silu_back(grad_cond)
    table_term = jnp.dot(jnp.transpose(grad_embed), step_hot, precision=HIGHEST)
    shares = (
        lax.psum_scatter(skip_weight_term, "blk", scatter_dimension=0, tiled=True),
        lax.psum_scatter(skip_bias_term, "blk", scatter_dimension=0, tiled=True),
        lax.psum_scatter(adaptive_weight_term, "blk", scatter_dimension=0, tiled=True),
        lax.psum_scatter(adaptive_bias_term, "blk", scatter_dimension=0, tiled=True),
        lax.psum_scatter(merged_weight_term, "blk", scatter_dimension=0, tiled=True),
        lax.psum_scatter(output_weight_term, "blk", scatter_dimension=0, tiled=True),
        lax.psum_scatter(output_bias_term, "blk", scatter_dimension=0, tiled=True),
        lax.psum_scatter(up_weight_term, "blk", scatter_dimension=0, tiled=True),
        lax.psum_scatter(up_bias_term, "blk", scatter_dimension=0, tiled=True),
        lax.psum_scatter(down_weight_term, "blk", scatter_dimension=0, tiled=True),
        lax.psum_scatter(down_bias_term, "blk", scatter_dimension=0, tiled=True),
        lax.psum_scatter(table_term, "blk", scatter_dimension=0, tiled=True),
    )
    summed = (
        lax.psum(shares[0].astype(jnp.bfloat16), "group").astype(jnp.float32),
        lax.psum(shares[1].astype(jnp.bfloat16), "group").astype(jnp.float32),
        lax.psum(shares[2].astype(jnp.bfloat16), "group").astype(jnp.float32),
        lax.psum(shares[3].astype(jnp.bfloat16), "group").astype(jnp.float32),
        lax.psum(shares[4].astype(jnp.bfloat16), "group").astype(jnp.float32),
        lax.psum(shares[5].astype(jnp.bfloat16), "group").astype(jnp.float32),
        lax.psum(shares[6].astype(jnp.bfloat16), "group").astype(jnp.float32),
        lax.psum(shares[7].astype(jnp.bfloat16), "group").astype(jnp.float32),
        lax.psum(shares[8].astype(jnp.bfloat16), "group").astype(jnp.float32),
        lax.psum(shares[9].astype(jnp.bfloat16), "group").astype(jnp.float32),
        lax.psum(shares[10].astype(jnp.bfloat16), "group").astype(jnp.float32),
        lax.psum(shares[11].astype(jnp.bfloat16), "group").astype(jnp.float32),
    )
    return (
        layer_out[None],
        frames_grad[None],
        skip_grad[None],
        jnp.transpose(summed[11]),
        summed[0],
        summed[1],
        summed[2],
        summed[3],
        summed[4],
        summed[5],
        summed[6],
        summed[7],
        summed[8],
        summed[9],
        summed[10],
    )


def solution(mesh):
    in_specs = (
        P("group", "blk", None),
        P("group", "blk", None),
        P("group", None),
        P("group", None),
        P("group", None),
        P(),
        P(),
        P(),
        P(),
        P(),
        P(),
        P(),
        P(),
        P(),
        P(),
        P(),
        P(),
        P("group", "blk", None),
    )
    out_specs = (
        P("group", "blk", None),
        P("group", "blk", None),
        P("group", "blk", None),
        P(None, "blk"),
        P("blk", None),
        P("blk"),
        P("blk", None),
        P("blk"),
        P("blk", None),
        P("blk", None),
        P("blk"),
        P("blk", None),
        P("blk"),
        P("blk", None),
        P("blk"),
    )
    return jax.shard_map(
        on_device, mesh=mesh, in_specs=in_specs, out_specs=out_specs, check_vma=False
    )
```

profile of v0, /device:TPU:13, one launch (start us, length us, event | category | flops | bytes accessed | tf_op | source)
XLA Modules:
  0.0 1715.3 jit_solution(10517567339517517295)
XLA Ops:
  29.5 42.3 %all-gather.5.cloned.1.call-done = bf16[1024,1024]{1,0:T(8,128)(2,1)} async-done(((bf16[128,1024]{1,0:T(8,128)(2,1)}), bf16[1024,1024]{1,0:T(8,128)(2,1)}) %all-gather.5.cloned.1.call-update) | async-done | bytes 2097168 | tf_op jit(solution)/shard_map/all_gather | solution.py:141
  75.7 47.2 %all-gather.7.cloned.1.call-done = bf16[1024,1024]{0,1:T(8,128)(2,1)} async-done(((bf16[128,1024]{0,1:T(8,128)(2,1)}), bf16[1024,1024]{0,1:T(8,128)(2,1)}) %all-gather.7.cloned.1.call-update) | async-done | bytes 2097168 | tf_op jit(solution)/shard_map/all_gather | solution.py:140
  122.9 10.7 while.52
  145.4 8.4 convert_reduce_fusion.3
  168.8 20.3 %while.53 = (s32[]{:T(128)}, f32[128,1024]{0,1:T(8,128)S(1)}, bf16[1024,1024]{0,1:T(8,128)(2,1)}, s32[128]{0:T(128)S(1)}, s32[8,1]{0,1:T(1,128)S(1)}, /*index=5*...) while((s32[]{:T(128)}, f32[128,1024]{0,1:T(8,128)S(1)}, ...), condition=%wide.region_20.21_spmd.clone, body=%wide.region_16.20_spmd.clone.sunk | while | flops 409371136 | bytes 18509616 | solution.py:65
  189.1 22.9 %all_gather.21 = f32[16,1024]{1,0:T(8,128)S(1)} all-gather(f32[16,128]{1,0:T(8,128)S(1)} %get-tuple-element.1533), channel_id=1, replica_groups=mesh['blk'=8,'group'=4] {'blk'}, dimensions={1}, use_global_device_ids=true | all-gather | bytes 73728 | tf_op jit(solution)/shard_map/all_gather | solution.py:228
  212.0 13.9 all-gather.11.cloned.1.call-done
  225.9 29.5 %while.54 = (s32[]{:T(128)}, f32[128,1024]{0,1:T(8,128)}, f32[128,1024]{0,1:T(8,128)}, bf16[1024,1024]{0,1:T(8,128)(2,1)}, s32[1,8]{1,0:T(1,128)}, /*index=5*/s3...) while((s32[]{:T(128)}, f32[128,1024]{0,1:T(8,128)}, ...), condition=%wide.region_25.26_spmd.clone, body=%wide.region_23.25_spmd.clone.sunk | while | flops 546975744 | bytes 46965944 | solution.py:65
  245.8 5.2 fusion.181
  270.6 6.3 fusion.50
  278.2 8.1 fusion.93
  288.0 8.1 fusion.52
  298.4 10.3 fusion.80
  308.8 8.9 fusion.91
  320.8 148.0 %reduce-scatter.10.cloned.1.call-done = f32[256,1024]{1,0:T(8,128)} async-done(((f32[2048,1024]{1,0:T(8,128)}), f32[256,1024]{1,0:T(8,128)}) %reduce-scatter.10.cloned.1.call-update) | async-done | bytes 1048592 | tf_op jit(solution)/shard_map/reduce_scatter | solution.py:290
  470.9 207.7 %reduce-scatter.14.cloned.1.call-done = f32[128,3072]{1,0:T(8,128)} async-done(((f32[1024,3072]{1,0:T(8,128)}), f32[128,3072]{1,0:T(8,128)}) %reduce-scatter.14.cloned.1.call-update) | async-done | bytes 1572880 | tf_op jit(solution)/shard_map/reduce_scatter | solution.py:294
  680.9 283.1 %reduce-scatter.18.cloned.1.call-done = f32[128,4096]{1,0:T(8,128)} async-done(((f32[1024,4096]{1,0:T(8,128)}), f32[128,4096]{1,0:T(8,128)}) %reduce-scatter.18.cloned.1.call-update) | async-done | bytes 2097168 | tf_op jit(solution)/shard_map/reduce_scatter | solution.py:297
  966.8 283.3 %reduce-scatter.20.cloned.1.call-done = f32[512,1024]{1,0:T(8,128)} async-done(((f32[4096,1024]{1,0:T(8,128)}), f32[512,1024]{1,0:T(8,128)}) %reduce-scatter.20.cloned.1.call-update) | async-done | bytes 2097168 | tf_op jit(solution)/shard_map/reduce_scatter | solution.py:299
  1252.8 282.7 %reduce-scatter.12.cloned.1.call-done = f32[128,4096]{1,0:T(8,128)} async-done(((f32[1024,4096]{1,0:T(8,128)}), f32[128,4096]{1,0:T(8,128)}) %reduce-scatter.12.cloned.1.call-update) | async-done | bytes 2097168 | tf_op jit(solution)/shard_map/reduce_scatter | solution.py:292
  1540.7 6.3 fusion.43
  1547.0 24.7 %all-reduce.5 = (bf16[1024]{0:T(1024)(128)(2,1)S(1)}, bf16[4096]{0:T(1024)(128)(2,1)S(1)}, bf16[1024]{0:T(1024)(128)(2,1)S(1)}, bf16[4096]{0:T(1024)(128)(2,1)S(1)}, bf16[1024]{0:T(1024)(128)(2,1)S(1)}) all-reduce(f32[1024]{0:T(1024)S(1)} %get-tuple-element.1053, ...), channel_id=4, replica_groups=mesh['blk'=8,'group'=4] {'blk'}, use_global_device_ids=true, to_apply=%region_33.34.clone | all-reduce | flops 11264 | bytes 67584
  1576.7 22.3 %reduce-scatter.8.cloned.1.call-done = f32[128,32]{0,1:T(8,128)} async-done(((f32[1024,32]{0,1:T(8,128)}), f32[128,32]{0,1:T(8,128)}) %reduce-scatter.8.cloned.1.call-update) | async-done | bytes 16400 | tf_op jit(solution)/shard_map/reduce_scatter | solution.py:301
  1599.7 12.0 all-reduce.6
  1615.0 84.1 %all-reduce.10.cloned.1.call-done = (bf16[256,1024]{1,0:T(8,128)(2,1)}, bf16[128,4096]{1,0:T(8,128)(2,1)}, bf16[128,3072]{1,0:T(8,128)(2,1)}, bf16[128,1024]{1,0...) async-done(((bf16[256,1024]{1,0:T(8,128)(2,1)}, bf16[128,4096]{1,0:T(8,128)(2,1)}, bf16[128,3072]{1,0:T(8,128)(2,1)}, bf16[128,1024]{1,0:T(8,128)(2,1)}, ...) | async-done | bytes 4718608 | tf_op jit(solution)/shard_map/psum | solution.py:304
  (342 shorter events, 162.6 us)
Async XLA Ops:
  7.2 126.5 %copy-start = (bf16[1024,1024]{1,0:T(8,128)(2,1)S(1)}, bf16[1024,1024]{1,0:T(8,128)(2,1)}, u32[]{:S(2)}) copy-start(bf16[1024,1024]{1,0:T(8,128)(2,1)} %param.35) | copy-start | bytes 6291460
  7.2 64.6 %all-gather.5.cloned.1.call-start = ((), (), s32[]{:S(2)}) async-start(), calls=%async_computation.7 | async-start | bytes 2359296 | tf_op jit(solution)/shard_map/all_gather | solution.py:141
  12.0 6.5 copy-start.6
  12.5 7.5 slice-start.2
  12.7 7.3 slice-start.3
  23.0 99.9 %all-gather.7.cloned.1.call-start = ((), (), s32[]{:S(2)}) async-start(), calls=%async_computation.8 | async-start | bytes 2359296 | tf_op jit(solution)/shard_map/all_gather | solution.py:140
  28.4 183.6 %all-gather.9.cloned.1.call-start = ((), (), s32[]{:S(2)}) async-start(), calls=%async_computation.9 | async-start | bytes 2359296 | tf_op jit(solution)/shard_map/all_gather | solution.py:229
  29.2 196.7 %all-gather.11.cloned.1.call-start = ((), (), s32[]{:S(2)}) async-start(), calls=%async_computation.10 | async-start | bytes 2359296 | tf_op jit(solution)/shard_map/all_gather | solution.py:230
  135.3 21.6 %copy-start.13 = (f32[128,1024]{1,0:T(8,128)}, f32[128,1024]{1,0:T(8,128)S(1)}, u32[]{:S(2)}) copy-start(f32[128,1024]{1,0:T(8,128)S(1)} %get-tuple-element.1094) | copy-start | bytes 1572868
  140.5 13.3 slice-start
  145.3 8.5 copy-start.17
  145.3 8.4 slice-start.1
  145.3 8.4 copy-start.3
  161.2 157.8 %reduce-scatter.16.cloned.1.call-start = ((), (), s32[]{:S(2)}) async-start(), calls=%async_computation.15 | async-start | bytes 4718592 | tf_op jit(solution)/shard_map/reduce_scatter | solution.py:295
  168.7 300.0 %reduce-scatter.10.cloned.1.call-start = ((), (), s32[]{:S(2)}) async-start(), calls=%async_computation.12 | async-start | bytes 9437184 | tf_op jit(solution)/shard_map/reduce_scatter | solution.py:290
  168.8 57.1 %copy-start.16 = (bf16[128,16,64]{0,2,1:T(8,128)(2,1)S(1)}, bf16[128,16,64]{0,2,1:T(8,128)(2,1)}, u32[]{:S(2)}) copy-start(bf16[128,16,64]{0,2,1:T(8,128)(2,1)} %maximum_convert_fusion) | copy-start | bytes 786436
  189.1 36.8 %copy-start.5 = (f32[128,1024]{0,1:T(8,128)}, f32[128,1024]{0,1:T(8,128)S(1)}, u32[]{:S(2)}) copy-start(f32[128,1024]{0,1:T(8,128)S(1)} %get-tuple-element.728) | copy-start | bytes 1572868
  269.7 408.8 %reduce-scatter.14.cloned.1.call-start = ((), (), s32[]{:S(2)}) async-start(), calls=%async_computation.14 | async-start | bytes 14155776 | tf_op jit(solution)/shard_map/reduce_scatter | solution.py:294
  277.0 687.1 %reduce-scatter.18.cloned.1.call-start = ((), (), s32[]{:S(2)}) async-start(), calls=%async_computation.16 | async-start | bytes 18874368 | tf_op jit(solution)/shard_map/reduce_scatter | solution.py:297
  286.4 963.7 %reduce-scatter.20.cloned.1.call-start = ((), (), s32[]{:S(2)}) async-start(), calls=%async_computation.17 | async-start | bytes 18874368 | tf_op jit(solution)/shard_map/reduce_scatter | solution.py:299
  296.2 1239.3 %reduce-scatter.12.cloned.1.call-start = ((), (), s32[]{:S(2)}) async-start(), calls=%async_computation.13 | async-start | bytes 18874368 | tf_op jit(solution)/shard_map/reduce_scatter | solution.py:292
  308.7 9.0 copy-start.58
  308.7 1290.3 %reduce-scatter.8.cloned.1.call-start = ((), (), s32[]{:S(2)}) async-start(), calls=%async_computation.11 | async-start | bytes 147456 | tf_op jit(solution)/shard_map/reduce_scatter | solution.py:301
  318.7 1380.3 %all-reduce.10.cloned.1.call-start = ((), (), s32[]{:S(2)}) async-start(), calls=%async_computation.18 | async-start | bytes 9437184 | tf_op jit(solution)/shard_map/psum | solution.py:304
  (68 other events, 182.8 us)
Sparse Core Ops, SparseCore 0:
  23.1 48.6 all-gather.4
  74.4 48.4 all-gather.6
  125.5 49.2 all-gather.8
  176.8 49.0 all-gather.10
  229.4 88.2 reduce-scatter.15
  321.6 147.1 reduce-scatter.9
  472.4 206.1 reduce-scatter.13
  682.3 281.6 reduce-scatter.17
  968.3 281.6 reduce-scatter.19
  1253.7 281.7 reduce-scatter.11
  1539.2 59.8 reduce-scatter.7
  1603.0 96.0 all-reduce.9
where the time goes:
time: 1720 us
  waiting for transfers between devices  1410 us (82%)
  matrix products  140 us (8%)
  blocking collectives  59.6 us (3%)
  other arithmetic  44.2 us (3%)
  local copies, waits for them, and re-layouts  38.2 us (2%)
    reduce_scatter x1, waiting for transfers between devices, on_device(): lax.psum_scatter(down_weight_term, 'blk', scatter_dimension=0, tiled=True)  283 us
    reduce_scatter x1, waiting for transfers between devices, on_device(): lax.psum_scatter(up_weight_term, 'blk', scatter_dimension=0, tiled=True)  283 us
    reduce_scatter x1, waiting for transfers between devices, on_device(): lax.psum_scatter(adaptive_weight_term, 'blk', scatter_dimension=0, tiled=...  283 us
    reduce_scatter x1, waiting for transfers between devices, on_device(): lax.psum_scatter(merged_weight_term, 'blk', scatter_dimension=0, tiled=True)  208 us
    reduce_scatter x1, waiting for transfers between devices, on_device(): lax.psum_scatter(skip_weight_term, 'blk', scatter_dimension=0, tiled=True)  148 us
    psum x1, waiting for transfers between devices, on_device(): lax.psum(shares[0].astype(jnp.bfloat16), 'group').astype(jnp.float32)  84.1 us
    all_gather x1, waiting for transfers between devices, on_device(): piece_keys = lax.all_gather(keys, 'blk', axis=0, tiled=True)  47.2 us
    all_gather x1, waiting for transfers between devices, on_device(): piece_values = lax.all_gather(values, 'blk', axis=0, tiled=True)  42.3 us
  transfers between devices with their start and end apart: 12, of which 10 were waited for; matrix products, arithmetic and copies ran while one was open for 11% of the time, Pallas kernels for 0%

commit v1 on v0

--- a/solution.py
+++ b/solution.py
@@ -1,12 +1,19 @@
+import functools
 import math
 
 import jax
 import jax.numpy as jnp
 from jax import lax
+from jax.experimental import pallas as pl
+from jax.experimental.pallas import tpu as pltpu
 from jax.sharding import PartitionSpec as P
 
 HEADS = 16
 HD = 64
+LANES = 128
+MESH_ID = pl.DeviceIdType.MESH
+VMEM_SPEC = pl.BlockSpec(memory_space=pltpu.VMEM)
+VMEM_LIMIT = 58 * 2**20
 
 
 EPSILON = 1e-06
@@ -333,6 +340,752 @@
     )
 
 
+def halves(array):
+    low = lax.broadcasted_iota(jnp.int32, array.shape, 1) < HD
+    zero = jnp.zeros_like(array)
+    return jnp.concatenate([jnp.where(low, array, zero), jnp.where(low, zero, array)], axis=0)
+
+
+def pick_halves(stacked):
+    rows = stacked.shape[0] // 2
+    low = lax.broadcasted_iota(jnp.int32, (rows, stacked.shape[1]), 1) < HD
+    return jnp.where(low, stacked[:rows], stacked[rows:])
+
+
+def nt_dot(left, right):
+    return lax.dot_general(
+        left, right, (((1,), (1,)), ((), ())), preferred_element_type=jnp.float32
+    )
+
+
+def tn_dot(left, right):
+    return lax.dot_general(
+        left, right, (((0,), (0,)), ((), ())), preferred_element_type=jnp.float32
+    )
+
+
+def enter(partners):
+    barrier = pltpu.get_barrier_semaphore()
+    for partner in partners:
+        pl.semaphore_signal(barrier, inc=1, device_id=partner, device_id_type=MESH_ID)
+    pl.semaphore_wait(barrier, len(partners))
+
+
+def remote(source, target, send_sem, recv_sem, partner):
+    return pltpu.make_async_remote_copy(
+        src_ref=source,
+        dst_ref=target,
+        send_sem=send_sem,
+        recv_sem=recv_sem,
+        device_id=partner,
+        device_id_type=MESH_ID,
+    )
+
+
+def attend_forward_kernel(
+    n,
+    q_ref,
+    k_ref,
+    v_ref,
+    segq_ref,
+    segk_ref,
+    mixed_ref,
+    rq_ref,
+    rk_ref,
+    rv_ref,
+    mh_ref,
+    rt_ref,
+    out_ref,
+    send_sem,
+    recv_sem,
+    back_send,
+    back_recv,
+):
+    b, g = lax.axis_index("blk"), lax.axis_index("group")
+    rows = q_ref.shape[0]
+    enter([((b + d) % n, g) for d in range(1, n)])
+
+    def columns(block):
+        return pl.ds(pl.multiple_of(block * LANES, LANES), LANES)
+
+    def band(block):
+        return pl.ds(pl.multiple_of(block * rows, rows), rows)
+
+    sent = []
+    for which, (source, target) in enumerate(((k_ref, rk_ref), (v_ref, rv_ref), (q_ref, rq_ref))):
+        for d in range(1, n):
+            p = (b + d) % n
+            copy = remote(
+                source.at[:, columns(p)],
+                target.at[band(b)],
+                send_sem.at[which, p],
+                recv_sem.at[which, b],
+                (p, g),
+            )
+            copy.start()
+            sent.append(copy)
+    for source, target in ((k_ref, rk_ref), (v_ref, rv_ref), (q_ref, rq_ref)):
+        target[band(b), :] = source[:, columns(b)]
+
+    def wait_in(which, source, target, d):
+        p = (b + n - d) % n
+        remote(
+            source.at[:, columns(p)],
+            target.at[band(p)],
+            send_sem.at[which, p],
+            recv_sem.at[which, p],
+            (p, g),
+        ).wait_recv()
+
+    for d in range(1, n):
+        wait_in(0, k_ref, rk_ref, d)
+        wait_in(1, v_ref, rv_ref, d)
+
+    def block_step(d, carry):
+        p = (b + n - d) % n
+
+        @pl.when(d > 0)
+        def _():
+            wait_in(2, q_ref, rq_ref, d)
+
+        query = halves(rq_ref[band(p), :] * jnp.asarray(0.125, jnp.bfloat16))
+        allow = segq_ref[band(p), :] == segk_ref[...]
+        allow = jnp.concatenate([allow, allow], axis=0)
+        expo = jnp.where(allow, jnp.exp(nt_dot(query, rk_ref[...])), 0.0)
+        total = jnp.sum(expo, axis=1, keepdims=True)
+        numer = jnp.dot(
+            expo.astype(jnp.bfloat16), rv_ref[...], preferred_element_type=jnp.float32
+        )
+        inverse = 1.0 / total
+        mixed = pick_halves(numer * inverse)
+        mh_ref[band(p), :] = mixed
+        rt_ref[band(p), :] = pick_halves(jnp.broadcast_to(inverse, numer.shape))
+        out_ref[band(p), :] = mixed.astype(jnp.bfloat16)
+
+        @pl.when(d > 0)
+        def _():
+            remote(
+                out_ref.at[band(p)],
+                mixed_ref.at[:, columns(b)],
+                back_send.at[p],
+                back_recv.at[b],
+                (p, g),
+            ).start()
+
+        return carry
+
+    def ordered(i, carry):
+        return block_step((i + 1) % n, carry)
+
+    lax.fori_loop(0, n, ordered, 0)
+    mixed_ref[:, columns(b)] = out_ref[band(b), :]
+    for copy in sent:
+        copy.wait_send()
+    for d in range(1, n):
+        p = (b + d) % n
+        copy = remote(
+            out_ref.at[band(p)],
+            mixed_ref.at[:, columns(p)],
+            back_send.at[p],
+            back_recv.at[p],
+            (p, g),
+        )
+        copy.wait_send()
+        copy.wait_recv()
+
+
+def attend_forward(queries, keys, values, seg_q, seg_k, n):
+    rows, width = queries.shape
+    seq = rows * n
+    low, full = jnp.bfloat16, jnp.float32
+    shapes = [((rows, width), low)] + [((seq, LANES), low)] * 3 + [((seq, LANES), full)] * 2
+    return pl.pallas_call(
+        functools.partial(attend_forward_kernel, n),
+        out_shape=[jax.ShapeDtypeStruct(*shape) for shape in shapes],
+        in_specs=[VMEM_SPEC] * 5,
+        out_specs=[VMEM_SPEC] * 6,
+        scratch_shapes=[
+            pltpu.VMEM((seq, LANES), low),
+            pltpu.SemaphoreType.DMA((3, n)),
+            pltpu.SemaphoreType.DMA((3, n)),
+            pltpu.SemaphoreType.DMA((n,)),
+            pltpu.SemaphoreType.DMA((n,)),
+        ],
+        compiler_params=pltpu.CompilerParams(
+            collective_id=0, has_side_effects=True, vmem_limit_bytes=VMEM_LIMIT
+        ),
+        name="attend_forward",
+    )(queries, keys, values, seg_q, seg_k)
+
+
+def turn_back(array, cosine, sine):
+    lane = lax.broadcasted_iota(jnp.int32, array.shape, 1) % HD
+    other = jnp.where(
+        lane < HD // 2,
+        pltpu.roll(array, LANES - HD // 2, 1),
+        pltpu.roll(array, HD // 2, 1),
+    )
+    return array * cosine + other * sine
+
+
+def attend_backward_kernel(
+    n,
+    gm_ref,
+    rq_ref,
+    rk_ref,
+    rv_ref,
+    mh_ref,
+    rt_ref,
+    segq_ref,
+    segk_ref,
+    cos_ref,
+    sin_ref,
+    merged_ref,
+    rg_ref,
+    gq_ref,
+    gk_ref,
+    gv_ref,
+    gk_acc,
+    gv_acc,
+    send_sem,
+    recv_sem,
+    back_send,
+    back_recv,
+):
+    b, g = lax.axis_index("blk"), lax.axis_index("group")
+    rows, width = gm_ref.shape
+    enter([((b + d) % n, g) for d in range(1, n)])
+
+    def columns(block, part=0):
+        return pl.ds(pl.multiple_of(part * width + block * LANES, LANES), LANES)
+
+    def band(block):
+        return pl.ds(pl.multiple_of(block * rows, rows), rows)
+
+    def incoming(p):
+        return remote(
+            gm_ref.at[:, columns(p)], rg_ref.at[band(p)], send_sem.at[p], recv_sem.at[p], (p, g)
+        )
+
+    def outward(part, source, p):
+        return remote(
+            source.at[band(p)],
+            merged_ref.at[:, columns(b, part)],
+            back_send.at[part, p],
+            back_recv.at[part, b],
+            (p, g),
+        )
+
+    for d in range(1, n):
+        p = (b + d) % n
+        remote(
+            gm_ref.at[:, columns(p)], rg_ref.at[band(b)], send_sem.at[p], recv_sem.at[b], (p, g)
+        ).start()
+    rg_ref[band(b), :] = gm_ref[:, columns(b)]
+    gk_acc[...] = jnp.zeros_like(gk_acc)
+    gv_acc[...] = jnp.zeros_like(gv_acc)
+
+    def block_step(i, carry):
+        d = i
+        p = (b + n - d) % n
+
+        @pl.when(d > 0)
+        def _():
+            incoming(p).wait_recv()
+
+        query = halves(rq_ref[band(p), :] * jnp.asarray(0.125, jnp.bfloat16))
+        allow = segq_ref[band(p), :] == segk_ref[...]
+        allow = jnp.concatenate([allow, allow], axis=0)
+        expo = jnp.where(allow, jnp.exp(nt_dot(query, rk_ref[...])), 0.0)
+        pull = rg_ref[band(p), :].astype(jnp.float32) * rt_ref[band(p), :]
+        product = pull * mh_ref[band(p), :]
+        low = lax.broadcasted_iota(jnp.int32, product.shape, 1) < HD
+        correction = -jnp.concatenate(
+            [
+                jnp.sum(jnp.where(low, product, 0.0), axis=1, keepdims=True),
+                jnp.sum(jnp.where(low, 0.0, product), axis=1, keepdims=True),
+            ],
+            axis=0,
+        )
+        pulls = halves(pull.astype(jnp.bfloat16))
+        slope = (expo * (nt_dot(pulls, rv_ref[...]) + correction)).astype(jnp.bfloat16)
+        grad_query = pick_halves(
+            jnp.dot(slope, rk_ref[...], preferred_element_type=jnp.float32)
+        )
+        gq_ref[band(p), :] = turn_back(
+            grad_query * 0.125, cos_ref[band(p), :], sin_ref[band(p), :]
+        ).astype(jnp.bfloat16)
+
+        @pl.when(d > 0)
+        def _():
+            outward(0, gq_ref, p).start()
+
+        gk_acc[...] += tn_dot(query, slope)
+        gv_acc[...] += tn_dot(pulls, expo.astype(jnp.bfloat16))
+        return carry
+
+    lax.fori_loop(0, n, block_step, 0)
+    gv_ref[...] = jnp.transpose(gv_acc[...]).astype(jnp.bfloat16)
+    for d in range(1, n):
+        outward(2, gv_ref, (b + d) % n).start()
+    gk_ref[...] = turn_back(jnp.transpose(gk_acc[...]), cos_ref[...], sin_ref[...]).astype(
+        jnp.bfloat16
+    )
+    for d in range(1, n):
+        outward(1, gk_ref, (b + d) % n).start()
+    for part, source in enumerate((gq_ref, gk_ref, gv_ref)):
+        merged_ref[:, columns(b, part)] = source[band(b), :]
+    for d in range(1, n):
+        p = (b + d) % n
+        incoming(p).wait_send()
+        for part, source in enumerate((gq_ref, gk_ref, gv_ref)):
+            copy = remote(
+                source.at[band(p)],
+                merged_ref.at[:, columns(p, part)],
+                back_send.at[part, p],
+                back_recv.at[part, p],
+                (p, g),
+            )
+            copy.wait_send()
+            copy.wait_recv()
+
+
+def attend_backward(grad_mixed, held, seg_q, seg_k, cosine, sine, n):
+    rows, width = grad_mixed.shape
+    seq = rows * n
+    low, full = jnp.bfloat16, jnp.float32
+    return pl.pallas_call(
+        functools.partial(attend_backward_kernel, n),
+        out_shape=jax.ShapeDtypeStruct((rows, 3 * width), low),
+        in_specs=[VMEM_SPEC] * 10,
+        out_specs=VMEM_SPEC,
+        scratch_shapes=[
+            pltpu.VMEM((seq, LANES), low),
+            pltpu.VMEM((seq, LANES), low),
+            pltpu.VMEM((seq, LANES), low),
+            pltpu.VMEM((seq, LANES), low),
+            pltpu.VMEM((LANES, seq), full),
+            pltpu.VMEM((LANES, seq), full),
+            pltpu.SemaphoreType.DMA((n,)),
+            pltpu.SemaphoreType.DMA((n,)),
+            pltpu.SemaphoreType.DMA((3, n)),
+            pltpu.SemaphoreType.DMA((3, n)),
+        ],
+        compiler_params=pltpu.CompilerParams(
+            collective_id=1, has_side_effects=True, vmem_limit_bytes=VMEM_LIMIT
+        ),
+        name="attend_backward",
+    )(grad_mixed, *held, seg_q, seg_k, cosine, sine)
+
+
+def weight_grad_kernel(kinds, n, m, *refs):
+    count = len(kinds)
+    xs, gs = refs[:count], refs[count : 2 * count]
+    small_ref, extra_ref = refs[2 * count : 2 * count + 2]
+    at = 2 * count + 2
+    outs = refs[at : at + count]
+    small_out, extra_out = refs[at + count : at + count + 2]
+    at += count + 2
+    x_all, g_all, y_out, y_in, z_out, z_in, own = (
+        refs[at + i * count : at + (i + 1) * count] for i in range(7)
+    )
+    at += 7 * count
+    (
+        s_in,
+        s_sum,
+        gather_send,
+        gather_recv,
+        y_send,
+        y_recv,
+        z_send,
+        z_recv,
+        last_send,
+        last_recv,
+        s_send,
+        s_recv,
+    ) = refs[at:]
+    b, g = lax.axis_index("blk"), lax.axis_index("group")
+    y, z = b % 2, b // 2
+    depth = n // 2
+    enter([(b, (g + d) % m) for d in range(1, m)] + [((b + d) % n, g) for d in range(1, n)])
+    part = small_ref.shape[1] // n
+
+    def chunk(index, size):
+        return pl.ds(pl.multiple_of(index * size, size), size)
+
+    gathers = {}
+    for t in range(count):
+        for side, (source, target) in enumerate(((xs[t], x_all[t]), (gs[t], g_all[t]))):
+            split = kinds[t] == (side == 0)
+            size = target.shape[2]
+            for d in range(1, m):
+                p = (g + d) % m
+                copy = remote(
+                    source.at[:, chunk(p, size)] if split else source,
+                    target.at[g],
+                    gather_send.at[t, side, d],
+                    gather_recv.at[t, side, d],
+                    (b, p),
+                )
+                copy.start()
+                gathers[t, side, d] = copy
+    smalls = []
+    for d in range(1, n):
+        p = (b + d) % n
+        copy = remote(
+            small_ref.at[:, chunk(p, part)], s_in.at[d], s_send.at[0, d], s_recv.at[0, d], (p, g)
+        )
+        copy.start()
+        smalls.append(copy)
+    for d in range(1, m):
+        copy = remote(
+            extra_ref, extra_out.at[g], s_send.at[1, d], s_recv.at[1, d], (b, (g + d) % m)
+        )
+        copy.start()
+        smalls.append(copy)
+    extra_out[g] = extra_ref[...]
+    for t in range(count):
+        for side, (source, target) in enumerate(((xs[t], x_all[t]), (gs[t], g_all[t]))):
+            split = kinds[t] == (side == 0)
+            size = target.shape[2]
+            target[g] = source[:, chunk(g, size)] if split else source[...]
+
+    y_copies, z_copies, last_copies = {}, {}, {}
+
+    def products(t):
+        for side in range(2):
+            for d in range(1, m):
+                gathers[t, side, d].wait_recv()
+        x_ref, g_ref = x_all[t], g_all[t]
+        deep = x_ref.shape[0] * x_ref.shape[1]
+        size = own[t].shape[1]
+
+        def product(block):
+            left = x_ref[:, :, chunk(block, size)].reshape(deep, size)
+            right = g_ref[...].reshape(deep, g_ref.shape[2])
+            return tn_dot(left, right)
+
+        for zi in (2, 1, 3, 0):
+            zp = (z + zi) % depth
+            y_out[t][zi] = product(zp * 2 + (1 - y)).astype(jnp.bfloat16)
+            copy = remote(
+                y_out[t].at[zi],
+                y_in[t].at[zi],
+                y_send.at[t, zi],
+                y_recv.at[t, zi],
+                (z * 2 + (1 - y), g),
+            )
+            copy.start()
+            y_copies[t, zi] = copy
+        for zi in (2, 1, 3, 0):
+            zp = (z + zi) % depth
+            own[t][zi] = product(zp * 2 + y)
+
+    def over_z(t):
+        for zi in (2, 1, 3):
+            zp = (z + zi) % depth
+            y_copies[t, zi].wait_recv()
+            z_out[t][zi] = (own[t][zi] + y_in[t][zi].astype(jnp.float32)).astype(jnp.bfloat16)
+            copy = remote(
+                z_out[t].at[zi],
+                z_in[t].at[zi],
+                z_send.at[t, zi],
+                z_recv.at[t, zi],
+                (zp * 2 + y, g),
+            )
+            copy.start()
+            z_copies[t, zi] = copy
+
+    def finish(t):
+        y_copies[t, 0].wait_recv()
+        total = own[t][0] + y_in[t][0].astype(jnp.float32)
+        for zi in (1, 3, 2):
+            z_copies[t, zi].wait_recv()
+            total = total + z_in[t][zi].astype(jnp.float32)
+        outs[t][g] = total.astype(jnp.bfloat16)
+        for d in range(1, m):
+            copy = remote(
+                outs[t].at[g],
+                outs[t].at[g],
+                last_send.at[t, d],
+                last_recv.at[t, d],
+                (b, (g + d) % m),
+            )
+            copy.start()
+            last_copies[t, d] = copy
+
+    for step in range(count + 2):
+        if step < count:
+            products(step)
+        if step == 0:
+            s_in[0] = small_ref[:, chunk(b, part)]
+            for d in range(1, n):
+                smalls[d - 1].wait_recv()
+            s_sum[...] = jnp.sum(s_in[...], axis=0).astype(jnp.bfloat16)
+            small_out[g, b] = s_sum[...]
+            for d in range(1, n):
+                copy = remote(
+                    s_sum, small_out.at[g, b], s_send.at[2, d], s_recv.at[2, d], ((b + d) % n, g)
+                )
+                copy.start()
+                smalls.append(copy)
+        if step == 1:
+            for d in range(1, n):
+                smalls[n - 1 + m - 1 + d - 1].wait_recv()
+            for d in range(1, m):
+                copy = remote(
+                    small_out.at[g],
+                    small_out.at[g],
+                    s_send.at[3, d],
+                    s_recv.at[3, d],
+                    (b, (g + d) % m),
+                )
+                copy.start()
+                smalls.append(copy)
+        if 0 <= step - 1 < count:
+            over_z(step - 1)
+        if 0 <= step - 2 < count:
+            finish(step - 2)
+    for copy in last_copies.values():
+        copy.wait_recv()
+    for copy in smalls[n - 1 : n - 1 + m - 1] + smalls[-(m - 1) :]:
+        copy.wait_recv()
+    for group in (gathers, y_copies, z_copies, last_copies):
+        for copy in group.values():
+            copy.wait_send()
+    for copy in smalls:
+        copy.wait_send()
+
+
+def weight_grads(tasks, small, extra, n, m):
+    low, full = jnp.bfloat16, jnp.float32
+    xs, gs, kinds = zip(*tasks)
+    depth = n // 2
+    outs, x_all, g_all, y_out, own = [], [], [], [], []
+    for left, right, split_left in tasks:
+        rows, inner = left.shape
+        outer = right.shape[1]
+        inner, outer = (inner // m, outer) if split_left else (inner, outer // m)
+        block = (inner // n, outer)
+        outs.append(jax.ShapeDtypeStruct((m, *block), low))
+        x_all.append(pltpu.VMEM((m, rows, inner), low))
+        g_all.append(pltpu.VMEM((m, rows, outer), low))
+        y_out.append(pltpu.VMEM((depth, *block), low))
+        own.append(pltpu.VMEM((depth, *block), full))
+    count = len(tasks)
+    part = small.shape[1] // n
+    outs.append(jax.ShapeDtypeStruct((m, n, small.shape[0], part), low))
+    outs.append(jax.ShapeDtypeStruct((m, *extra.shape), low))
+    sems = [pltpu.SemaphoreType.DMA((count, 2, m))] * 2
+    sems += [pltpu.SemaphoreType.DMA((count, depth))] * 4
+    sems += [pltpu.SemaphoreType.DMA((count, m))] * 2
+    sems += [pltpu.SemaphoreType.DMA((4, max(n, m)))] * 2
+    return pl.pallas_call(
+        functools.partial(weight_grad_kernel, kinds, n, m),
+        out_shape=outs,
+        in_specs=[VMEM_SPEC] * (2 * count + 2),
+        out_specs=[VMEM_SPEC] * (count + 2),
+        scratch_shapes=x_all
+        + g_all
+        + y_out * 4
+        + own
+        + [
+            pltpu.VMEM((n, small.shape[0], part), full),
+            pltpu.VMEM((small.shape[0], part), low),
+        ]
+        + sems,
+        compiler_params=pltpu.CompilerParams(
+            collective_id=2, has_side_effects=True, vmem_limit_bytes=VMEM_LIMIT
+        ),
+        name="weight_grads",
+    )(*xs, *gs, small, extra)
+
+
+def by_heads(
+    n,
+    m,
+    frames,
+    skip_in,
+    lengths,
+    voiced,
+    time_steps,
+    time_table,
+    skip_weight,
+    skip_bias,
+    adaptive_weight,
+    adaptive_bias,
+    merged_weight,
+    output_weight,
+    output_bias,
+    up_weight,
+    up_bias,
+    down_weight,
+    down_bias,
+    cotangent,
+):
+    rows, width = frames.shape[1:]
+    ff = up_weight.shape[1]
+    low, full = jnp.bfloat16, jnp.float32
+    b, g = lax.axis_index("blk"), lax.axis_index("group")
+    everywhere = jnp.arange(rows * n, dtype=jnp.int32)
+    segment, offset, valid, member_all = frame_facts(lengths[0], voiced[0], everywhere)
+    cosine_all, sine_all = turn_tables(offset, HD)
+    seg_q = segment.astype(full)[:, None]
+    seg_k = jnp.where(valid, segment, -1).astype(full)[None, :]
+    cos_lanes = jnp.tile(cosine_all, (1, LANES // cosine_all.shape[1]))
+    sin_lanes = jnp.tile(
+        jnp.concatenate([sine_all, -sine_all], axis=1), (1, LANES // (2 * sine_all.shape[1]))
+    )
+    cosine = lax.dynamic_slice_in_dim(cosine_all, b * rows, rows, 0)
+    sine = lax.dynamic_slice_in_dim(sine_all, b * rows, rows, 0)
+    member = lax.dynamic_slice_in_dim(member_all, b * rows, rows, 0)
+
+    step_hot = (
+        time_steps[0][:, None] == jnp.arange(time_table.shape[0], dtype=jnp.int32)[None, :]
+    ).astype(full)
+    embed = jnp.dot(step_hot, time_table.astype(full), precision=HIGHEST)
+    cond_low = jax.nn.silu(embed).astype(low)
+    per_utterance = jnp.dot(
+        cond_low, adaptive_weight, preferred_element_type=full
+    ) + adaptive_bias.astype(full)
+    modulate = jnp.dot(member, per_utterance, precision=HIGHEST)
+    joined = jnp.concatenate([frames[0], skip_in[0]], axis=1)
+    first = jnp.dot(joined, skip_weight, preferred_element_type=full) + skip_bias.astype(full)
+    normed, norm_back = jax.vjp(
+        adaptive_norm, first, modulate[:, :width], modulate[:, width : 2 * width]
+    )
+    normed_low = normed.astype(low)
+    merged = jnp.dot(normed_low, merged_weight, preferred_element_type=full)
+
+    def turned(part):
+        heads = part.reshape(rows, HEADS, HD)
+        return rotate(heads, cosine, sine).astype(low).reshape(rows, width)
+
+    queries = turned(merged[:, :width])
+    keys = turned(merged[:, width : 2 * width])
+    values = merged[:, 2 * width :].astype(low)
+    mixed_low, *held = attend_forward(queries, keys, values, seg_q, seg_k, n)
+
+    attended = jnp.dot(mixed_low, output_weight, preferred_element_type=full) + output_bias.astype(
+        full
+    )
+    second = first + attended
+    normed_two, norm_two_back = jax.vjp(
+        adaptive_norm, second, modulate[:, 2 * width : 3 * width], modulate[:, 3 * width :]
+    )
+    normed_two_low = normed_two.astype(low)
+    hidden = jnp.dot(normed_two_low, up_weight, preferred_element_type=full) + up_bias.astype(full)
+    activated, gelu_back = jax.vjp(jax.nn.gelu, hidden)
+    activated_low = activated.astype(low)
+    result = (
+        second
+        + jnp.dot(activated_low, down_weight, preferred_element_type=full)
+        + down_bias.astype(full)
+    )
+    layer_out = result.astype(low)
+    outer_grad = cotangent[0]
+    outer_float = outer_grad.astype(full)
+    grad_act = jnp.einsum("rd,fd->rf", outer_grad, down_weight, preferred_element_type=full)
+    (grad_hidden,) = gelu_back(grad_act)
+    grad_hidden_low = grad_hidden.astype(low)
+    grad_normed_two = jnp.einsum(
+        "rf,df->rd", grad_hidden_low, up_weight, preferred_element_type=full
+    )
+    grad_second_norm, grad_scale_two, grad_shift_two = norm_two_back(grad_normed_two)
+    grad_second = outer_float + grad_second_norm
+    grad_attended = grad_second.astype(low)
+    grad_mixed = jnp.einsum(
+        "re,de->rd", grad_attended, output_weight, preferred_element_type=full
+    ).astype(low)
+    grad_merged = attend_backward(grad_mixed, held, seg_q, seg_k, cos_lanes, sin_lanes, n)
+    grad_normed = jnp.einsum("re,de->rd", grad_merged, merged_weight, preferred_element_type=full)
+    grad_first_norm, grad_scale_one, grad_shift_one = norm_back(grad_normed)
+    grad_first = (grad_second + grad_first_norm).astype(low)
+    grad_joined = jnp.einsum("rd,cd->rc", grad_first, skip_weight, preferred_element_type=full)
+    frames_grad = grad_joined[:, :width].astype(low)
+    skip_grad = grad_joined[:, width:].astype(low)
+
+    frame_modulate = jnp.concatenate(
+        [grad_scale_one, grad_shift_one, grad_scale_two, grad_shift_two], axis=1
+    )
+    grad_modulate = jnp.dot(jnp.transpose(member), frame_modulate, precision=HIGHEST)
+    utterances = grad_modulate.shape[0]
+    biases = jnp.concatenate(
+        [
+            jnp.sum(grad_hidden_low.astype(full), axis=0),
+            jnp.sum(grad_first.astype(full), axis=0),
+            jnp.sum(grad_attended.astype(full), axis=0),
+            jnp.sum(outer_float, axis=0),
+            jnp.zeros((width,), full),
+        ]
+    ).reshape(2, 4 * width)
+    small = jnp.concatenate([grad_modulate, biases, jnp.zeros((6, 4 * width), full)], axis=0)
+    extra = jnp.concatenate([embed, step_hot, jnp.zeros((utterances, 96), full)], axis=1)
+    extra = jnp.concatenate([extra, jnp.zeros_like(extra)], axis=0).astype(low)
+
+    quarter = ff // (n * m)
+    activated_turned = (
+        activated_low.reshape(rows, n, m, quarter).transpose(0, 2, 1, 3).reshape(rows, ff)
+    )
+    *terms, small_all, extra_all = weight_grads(
+        (
+            (activated_turned, outer_grad, True),
+            (normed_two_low, grad_hidden_low, False),
+            (mixed_low, grad_attended, False),
+            (normed_low, grad_merged, False),
+            (joined, grad_first, False),
+        ),
+        small,
+        extra,
+        n,
+        m,
+    )
+    down_grad = terms[0].astype(full).reshape(-1, width)
+    up_grad, output_grad, merged_grad, skip_grad_weight = (
+        jnp.transpose(term, (1, 0, 2)).reshape(term.shape[1], -1).astype(full) for term in terms[1:]
+    )
+    small_all = jnp.transpose(small_all, (0, 2, 1, 3)).reshape(m, small.shape[0], 4 * width)
+    modulate_low = small_all[:, :utterances].reshape(m * utterances, 4 * width)
+    bias_sums = jnp.sum(small_all[:, utterances : utterances + 2].astype(full), axis=0).reshape(-1)
+    embed_all = extra_all[:, :utterances, :width].reshape(m * utterances, width).astype(full)
+    hot_all = extra_all[:, :utterances, width : width + time_table.shape[0]].reshape(
+        m * utterances, -1
+    )
+    share = width // n
+    embed_here = lax.dynamic_slice_in_dim(embed_all, b * share, share, 1)
+    cond_here, silu_back = jax.vjp(jax.nn.silu, embed_here)
+    adaptive_weight_grad = jnp.einsum(
+        "ur,uc->rc", cond_here.astype(low), modulate_low, preferred_element_type=full
+    )
+    adaptive_bias_sums = jnp.sum(modulate_low.astype(full), axis=0)
+    weight_here = lax.dynamic_slice_in_dim(adaptive_weight, b * share, share, 0)
+    grad_cond = jnp.einsum("uc,rc->ur", modulate_low, weight_here, preferred_element_type=full)
+    (grad_embed,) = silu_back(grad_cond)
+    table_grad = jnp.dot(jnp.transpose(hot_all.astype(full)), grad_embed, precision=HIGHEST)
+
+    def own_part(vector):
+        size = vector.shape[0] // n
+        return lax.dynamic_slice_in_dim(vector, b * size, size, 0)
+
+    return (
+        layer_out[None],
+        frames_grad[None],
+        skip_grad[None],
+        table_grad,
+        skip_grad_weight,
+        own_part(bias_sums[4 * width : 5 * width]),
+        adaptive_weight_grad,
+        own_part(adaptive_bias_sums),
+        merged_grad,
+        output_grad,
+        own_part(bias_sums[5 * width : 6 * width]),
+        up_grad,
+        own_part(bias_sums[: 4 * width]),
+        down_grad,
+        own_part(bias_sums[6 * width : 7 * width]),
+    )
+
+
 def solution(mesh):
     in_specs = (
         P("group", "blk", None),
@@ -371,6 +1124,9 @@
         P("blk", None),
         P("blk"),
     )
+    n, m = mesh.shape["blk"], mesh.shape["group"]
+    fits = n % 2 == 0 and n // 2 == 4 and n * LANES == HEADS * HD and m == 4
+    body = functools.partial(by_heads, n, m) if fits else on_device
     return jax.shard_map(
-        on_device, mesh=mesh, in_specs=in_specs, out_specs=out_specs, check_vma=False
-    )
+        body, mesh=mesh, in_specs=in_specs, out_specs=out_specs, check_vma=False
+    )

time: 1720 us -> 338 us (0.20)
  waiting for transfers between devices: 1410 us -> 0 us
  Pallas kernels: 0 us -> 223 us
  matrix products: 140 us -> 47.6 us
  blocking collectives: 59.6 us -> 0 us
  other arithmetic: 44.2 us -> 17.7 us
    reduce_scatter x7 -> x0, waiting for transfers between devices: 1230 us -> none  [the longest x1 283 us: on_device(): lax.psum_scatter(down_weight_term, 'blk', scatter_dimension=0, tiled=True)]
    pallas_call x0 -> x3, Pallas kernels: none -> 223 us  [the longest x1 162 us: weight_grads(): pl.pallas_call(functools.partial(weight_grad_kernel, kinds, n, m), out_sh...]
    all_gather x4 -> x0, waiting for transfers between devices: 103 us -> none  [the longest x1 47.2 us: on_device(): piece_keys = lax.all_gather(keys, 'blk', axis=0, tiled=True)]
    dot_general x36 -> x17, matrix products: 140 us -> 47.6 us  [the longest x1 6.8 us: by_heads(): jnp.dot(normed_two_low, up_weight, preferred_element_type=full)]
    psum x1 -> x0, waiting for transfers between devices: 84.1 us -> none  [on_device(): lax.psum(shares[0].astype(jnp.bfloat16), 'group').astype(jnp.float32)]
    convert_element_type x28 -> x13, other arithmetic: 31.6 us -> 5.98 us  [the longest x4 4.18 us: by_heads(): jnp.transpose(term, (1, 0, 2)).reshape(term.shape[1], -1).astype(full)]
    unnamed x1 -> x0, blocking collectives: 24.7 us -> none
    all_gather x1 -> x0, blocking collectives: 22.9 us -> none  [on_device(): corrections_all = lax.all_gather(correction, 'blk', axis=1, tiled=True)]
  transfers between devices with their start and end apart: 12 -> 0, of which waited for: 10 -> 0; matrix products, arithmetic and copies ran while one was open for 11% -> 0% of each run, Pallas kernels for 0% -> 0%
where the time goes in v1:
time: 338 us; the launch traced here: 336 us
  Pallas kernels  223 us (66%)
  matrix products  47.6 us (14%)
  local copies, waits for them, and re-layouts  46.4 us (14%)
  other arithmetic  17.7 us (5%)
    pallas_call x1, Pallas kernels, weight_grads(): pl.pallas_call(functools.partial(weight_grad_kernel, kinds, n, m), out_sh...  162 us
    pallas_call x1, Pallas kernels, attend_backward(): pl.pallas_call(functools.partial(attend_backward_kernel, n), out_shape=ja...  32.4 us
    pallas_call x1, Pallas kernels, attend_forward(): pl.pallas_call(functools.partial(attend_forward_kernel, n), out_shape=[ja...  28.7 us
    unnamed x113, local copies, waits for them, and re-layouts  14.9 us
    convert_element_type x4, local copies, waits for them, and re-layouts, by_heads(): jnp.transpose(term, (1, 0, 2)).reshape(term.shape[1], -1).astype(full)  7.41 us
    dot_general x1, matrix products, by_heads(): jnp.dot(normed_two_low, up_weight, preferred_element_type=full)  6.8 us

profile of v1, /device:TPU:13, one launch (start us, length us, event | category | flops | bytes accessed | tf_op | source)
XLA Modules:
  0.0 335.8 jit_solution(945476929544250791)
XLA Ops:
  1.5 3.2 fusion.77
  5.6 4.6 %convolution_add_fusion.1 = f32[8,4096]{1,0:T(8,128)S(1)} fusion(bf16[1024,4096]{1,0:T(8,128)(2,1)} %param.26, f32[4096]{0:T(1024)S(1)} %convert_element_type.163, f32[8,1024]{1,0:T(8,128)S(1)} %get-tuple-element.113), kind=kOutput, calls=%fused_computation.1 | convolution fusion | flops 67182592 | bytes 8568832 | tf_op jit(solution)/shard_map/dot_general | solution.py:948
  13.0 3.9 %fusion.80 = f32[128,3072]{1,0:T(8,128)S(1)} fusion(bf16[128,1024]{1,0:T(8,128)(2,1)S(1)} %fusion.22.refs_3_, bf16[1024,3072]{1,0:T(8,128)(2,1)} %param.28), kind=kOutput, calls=%fused_computation.157 | convolution fusion | flops 805306368 | bytes 8126464 | tf_op jit(solution)/shard_map/dot_general | solution.py:958
  22.4 2.0 copy.52
  24.4 1.9 subtract_convert_fusion
  32.3 28.7 %attend_forward.1 = (bf16[128,1024]{1,0:T(8,128)(2,1)}, bf16[1024,128]{1,0:T(8,128)(2,1)}, bf16[1024,128]{1,0:T(8,128)(2,1)}, bf16[1024,128]{1,0:T(8,128)(2,1)},...) custom-call(bf16[128,1024]{1,0:T(8,128)(2,1)} %copy.54.q_ref, bf16[128,1024]{1,0:T(8,128)(2,1)} %copy.55.k_ref, ...), custom_call_target="tpu_custom_call" | custom-call | tf_op jit(solution)/shard_map/attend_forward/pallas_call | solution.py:502
  63.1 6.8 %multiply_convert_fusion = (bf16[128,4096]{1,0:T(8,128)(2,1)S(1)}, f32[128,4096]{1,0:T(8,128)}) fusion(f32[4096]{0:T(1024)S(1)} %convert_element_type.173, bf16[128,1024]{1,0:T(8,128)(2,1)S(1)} %fusion.21.refs_1_, bf16[1024,4096]{1,0:T(8,128)(2,1)} %param.31), kind=kOutput, calls=%fused_computation.22 | convolution fusion | flops 1078984704 | bytes 11812864 | tf_op jit(solution)/shard_map/dot_general | solution.py:977
  70.0 2.0 fusion.18
  72.0 5.8 %convert_reduce_fusion = (f32[4096]{0:T(1024)}, bf16[128,4096]{1,0:T(8,128)(2,1)S(1)}) fusion(f32[128,4096]{1,0:T(8,128)} %get-tuple-element.105, bf16[4096,1024]{1,0:T(8,128)(2,1)S(1)} %bitcast.100, bf16[1,128,1024]{2,1,0:T(8,128)(2,1)S(1)} %copy-done.14), kind=kOutput, calls=%fused_computation.21 | convolution fusion | flops 1085272064 | bytes 11812864 | tf_op jit(solution)/shard_map/rd,fd->rf/dot_general | solution.py:988
  77.8 3.0 multiply_reduce_fusion.1
  84.4 2.0 copy.58.cos_ref
  88.3 2.0 copy.59.sin_ref
  90.3 32.4 %attend_backward.1.refs_8_ = bf16[128,3072]{1,0:T(8,128)(2,1)} custom-call(bf16[128,1024]{1,0:T(8,128)(2,1)} %convolution_convert_fusion.1.gm_ref, bf16[1024,128]{1,0:T(8,128)(2,1)} %get-tuple-element.29.rq_ref, bf16[1024,128]{1,0:T(8,128)(2,1)} %get-tuple-element.30.rk_ref, bf16[1024,128]{1,0:T(8,128)(2,1)} %get-tuple-element.31.rv_ref, ...), custom_call_target="tpu_custom_call" | custom-call | tf_op jit(solution)/shard_map/attend_backward/pallas_call | solution.py:657
  122.8 5.4 %multiply_reduce_fusion = (f32[128]{0:T(128)S(1)}, f32[128,1024]{1,0:T(8,128)S(1)}) fusion(f32[128,1024]{1,0:T(8,128)S(1)} %get-tuple-element.101, f32[128]{0:T(128)S(1)} %copy-done.36, f32[128,4096]{1,0:T(8,128)S(1)} %copy-done.3, bf16[128,3072]{1,0:T(8,128)(2,1)} %attend_backward.1.refs_8_, bf16[1024,3072]{1,0:T(8,128)(2,1)} %param.28), kind=kOutput, calls=%fused_computation.54 | convolution fusion | flops 805961600 | bytes 8651776 | tf_op jit(solution)/shard_map/re,de->rd/dot_general | solution.py:1001
  138.6 2.0 fusion.7
  142.3 161.7 %weight_grads.1 = (bf16[4,128,1024]{2,1,0:T(8,128)(2,1)}, bf16[4,128,1024]{2,1,0:T(8,128)(2,1)}, bf16[4,128,256]{2,1,0:T(8,128)(2,1)}, bf16[4,128,768]{2,1,0:T(8...) custom-call(bf16[128,4096]{1,0:T(8,128)(2,1)} %bitcast.108, ...), custom_call_target="tpu_custom_call" | custom-call | tf_op jit(solution)/shard_map/weight_grads/pallas_call | solution.py:883
  305.2 1.9 fusion.19
  309.3 2.6 copy.66
  312.6 1.8 fusion.26
  316.4 3.0 copy.63
  319.4 3.1 copy.67
  324.3 2.8 convert_bitcast_fusion
  327.1 2.9 copy.65
  330.0 3.0 copy.69
  (190 shorter events, 46.0 us)
Async XLA Ops:
  0.6 60.4 %copy-start = (bf16[1024,1024]{1,0:T(8,128)(2,1)S(1)}, bf16[1024,1024]{1,0:T(8,128)(2,1)}, u32[]{:S(2)}) copy-start(bf16[1024,1024]{1,0:T(8,128)(2,1)} %param.29) | copy-start | bytes 6291460
  1.5 3.3 copy-start.39
  5.6 4.6 %copy-start.46 = (s32[1,8]{1,0:T(1,128)S(1)}, s32[1,8]{1,0:T(1,128)}, u32[]{:S(2)}) copy-start(s32[1,8]{1,0:T(1,128)} %param.20) | copy-start | bytes 100
  11.5 5.4 %copy-start.35 = (f32[128]{0:T(128)}, f32[128]{0:T(128)S(1)}, u32[]{:S(2)}) copy-start(f32[128]{0:T(128)S(1)} %broadcast_multiply_fusion.1) | copy-start | bytes 1540
  11.7 5.2 %copy-start.44 = (f32[128]{0:T(128)}, f32[128]{0:T(128)S(1)}, u32[]{:S(2)}) copy-start(f32[128]{0:T(128)S(1)} %multiply_reduce_fusion.3) | copy-start | bytes 1540
  12.8 4.1 %copy-start.37 = (f32[128]{0:T(128)}, f32[128]{0:T(128)S(1)}, u32[]{:S(2)}) copy-start(f32[128]{0:T(128)S(1)} %fusion.62) | copy-start | bytes 1540
  13.0 3.9 %copy-start.9 = (bf16[128,1024]{1,0:T(8,128)(2,1)}, bf16[128,1024]{1,0:T(8,128)(2,1)S(1)}, u32[]{:S(2)}) copy-start(bf16[128,1024]{1,0:T(8,128)(2,1)S(1)} %fusion.22.refs_3_) | copy-start | bytes 786436
  21.7 6.4 %copy-start.25 = (f32[1024,32]{0,1:T(8,128)}, f32[1024,32]{0,1:T(8,128)S(1)}, u32[]{:S(2)}) copy-start(f32[1024,32]{0,1:T(8,128)S(1)} %get-tuple-element.98) | copy-start | bytes 393220
  32.3 30.3 %copy-start.34 = (bf16[4096]{0:T(1024)(128)(2,1)S(1)}, bf16[4096]{0:T(1024)(128)(2,1)}, u32[]{:S(2)}) copy-start(bf16[4096]{0:T(1024)(128)(2,1)} %param.32) | copy-start | bytes 24580
  62.9 7.0 %slice-start = ((s8[8388608]{0:T(1024)(128)(4,1)}), s8[4194304]{0:T(1024)(128)(4,1)S(1)}, s32[]{:S(2)}) async-start(s8[8388608]{0:T(1024)(128)(4,1)} %bitcast.99), calls=%async_computation | async-start | bytes 8388608
  63.1 6.8 %copy-start.21 = (bf16[128,1024]{1,0:T(8,128)(2,1)}, bf16[128,1024]{1,0:T(8,128)(2,1)S(1)}, u32[]{:S(2)}) copy-start(bf16[128,1024]{1,0:T(8,128)(2,1)S(1)} %fusion.21.refs_1_) | copy-start | bytes 786436
  63.1 6.8 %copy-start.42 = (bf16[1024]{0:T(1024)(128)(2,1)S(1)}, bf16[1024]{0:T(1024)(128)(2,1)}, u32[]{:S(2)}) copy-start(bf16[1024]{0:T(1024)(128)(2,1)} %param.34) | copy-start | bytes 6148
  63.1 6.8 %slice-start.1 = ((s8[8388608]{0:T(1024)(128)(4,1)}), s8[4194304]{0:T(1024)(128)(4,1)S(1)}, s32[]{:S(2)}) async-start(s8[8388608]{0:T(1024)(128)(4,1)} %bitcast.99), calls=%async_computation.1 | async-start | bytes 8388608
  70.0 7.8 %slice-start.2 = ((s8[8388608]{0:T(1024)(128)(4,1)}), s8[4194304]{0:T(1024)(128)(4,1)S(1)}, s32[]{:S(2)}) async-start(s8[8388608]{0:T(1024)(128)(4,1)} %bitcast.101), calls=%async_computation.2 | async-start | bytes 8388608
  72.0 5.8 %slice-start.3 = ((s8[8388608]{0:T(1024)(128)(4,1)}), s8[4194304]{0:T(1024)(128)(4,1)S(1)}, s32[]{:S(2)}) async-start(s8[8388608]{0:T(1024)(128)(4,1)} %bitcast.101), calls=%async_computation.3 | async-start | bytes 8388608
  82.0 4.4 %copy-start.12 = (bf16[128,1024]{1,0:T(8,128)(2,1)}, bf16[128,1024]{1,0:T(8,128)(2,1)S(1)}, u32[]{:S(2)}) copy-start(bf16[128,1024]{1,0:T(8,128)(2,1)S(1)} %get-tuple-element.74.refs_7_) | copy-start | bytes 786436
  90.3 32.4 %copy-start.3 = (f32[128,4096]{1,0:T(8,128)S(1)}, f32[128,4096]{1,0:T(8,128)}, u32[]{:S(2)}) copy-start(f32[128,4096]{1,0:T(8,128)} %copy-done.1) | copy-start | bytes 6291460
  90.3 32.4 %copy-start.36 = (f32[128]{0:T(128)S(1)}, f32[128]{0:T(128)}, u32[]{:S(2)}) copy-start(f32[128]{0:T(128)} %copy-done.35) | copy-start | bytes 1540
  122.7 5.4 %copy-start.45 = (f32[128]{0:T(128)S(1)}, f32[128]{0:T(128)}, u32[]{:S(2)}) copy-start(f32[128]{0:T(128)} %copy-done.44) | copy-start | bytes 1540
  122.7 5.5 %copy-start.38 = (f32[128]{0:T(128)S(1)}, f32[128]{0:T(128)}, u32[]{:S(2)}) copy-start(f32[128]{0:T(128)} %copy-done.37) | copy-start | bytes 1540
  122.7 6.5 %copy-start.15 = (bf16[1,128,1024]{2,1,0:T(8,128)(2,1)S(1)}, bf16[1,128,1024]{2,1,0:T(8,128)(2,1)}, u32[]{:S(2)}) copy-start(bf16[1,128,1024]{2,1,0:T(8,128)(2,1)} %param.35) | copy-start | bytes 786436
  304.0 3.9 %copy-start.26 = (bf16[4,256,256]{2,1,0:T(8,128)(2,1)S(1)}, bf16[4,256,256]{2,1,0:T(8,128)(2,1)}, u32[]{:S(2)}) copy-start(bf16[4,256,256]{2,1,0:T(8,128)(2,1)} %get-tuple-element.36) | copy-start | bytes 1572868
  309.3 5.8 %copy-start.24 = (bf16[4,128,768]{2,1,0:T(8,128)(2,1)S(1)}, bf16[4,128,768]{2,1,0:T(8,128)(2,1)}, u32[]{:S(2)}) copy-start(bf16[4,128,768]{2,1,0:T(8,128)(2,1)} %get-tuple-element.37) | copy-start | bytes 2359300
  330.0 3.6 %copy-start.20 = (bf16[4,128,1024]{2,1,0:T(8,128)(2,1)S(1)}, bf16[4,128,1024]{2,1,0:T(8,128)(2,1)}, u32[]{:S(2)}) copy-start(bf16[4,128,1024]{2,1,0:T(8,128)(2,1)} %get-tuple-element.40) | copy-start | bytes 3145732
  (27 other events, 68.3 us)
